TPU v7x, 32 devices: a whole 2x2x4 slice. The times are simulated.
32 devices in a mesh: head: 4 (over y, x), tile: 8 (over z, core).
Axes of the slice: x: 2, y: 2, z: 4, core: 2. Of those that a mesh axis runs over, the one named last changes fastest.
Arguments:
- hidden: bfloat16 [8, 384, 1536], P(None, ('head', 'tile')), may hold values from -6 to 6
- latent: float32 [8, 384, 64], P(None, ('head', 'tile')), may hold values from -6 to 6
- cell_map: int32 [8, 384], P(None, ('head', 'tile')), may hold values from 0 to 383, each once within a row
- text_lengths: int32 [8], P('tile'), may hold values from 64 to 512, as said below
- block_modulation: float32 [8, 3, 1536], replicated, may hold values from -3 to 3
- head_modulation: float32 [8, 2, 1536], replicated, may hold values from -3 to 3
- step_sizes: float32 [8], replicated, may hold values from -0.5 to -0.1
- w_qkv: bfloat16 [1536, 4608], replicated, may hold values from -0.15625 to 0.15625
- self_q_gain: float32 [1536], replicated, may hold values from 0.5 to 2
- self_k_gain: float32 [1536], replicated, may hold values from 0.5 to 2
- w_out: bfloat16 [1536, 1536], replicated, may hold values from -0.15625 to 0.15625
- cross_gain: float32 [1536], replicated, may hold values from 0.1 to 1.9
- cross_wq: bfloat16 [1536, 1536], P(None, 'head'), may hold values from -0.15625 to 0.15625
- cross_q_gain: float32 [1536], P('head'), may hold values from 0.5 to 2
- text_keys: bfloat16 [8, 512, 1536], P('tile', None, 'head'), may hold values from -2.5 to 2.5
- text_values: bfloat16 [8, 512, 1536], P('tile', None, 'head'), may hold values from -4 to 4
- cross_wo: bfloat16 [1536, 1536], P('head'), may hold values from -0.15625 to 0.15625
- head_w: bfloat16 [1536, 64], replicated, may hold values from -0.15625 to 0.15625
Outputs:
- hidden_next: bfloat16 [8, 384, 1536], P(None, ('head', 'tile'))
- latent_next: float32 [8, 384, 64], P(None, ('head', 'tile'))
Inputs may be any that keep to these rules, and one draw needn't show every extreme that they name: Each row cell_map[v] names every cell of video v once. Text positions from text_lengths[v] on are padding of video v.
All inputs are finite; a program needn't handle non-finite values.
Results may differ from a plain program's by a relative error of at most 0.007.
Values may be sent and summed in bfloat16 or wider, within the bound.
A program may use at most 128 MiB of HBM per device.

v0:
```python
import math

import jax
import jax.numpy as jnp
from jax import lax
from jax.sharding import PartitionSpec as P

HEADS = 12
HEAD_DIM = 128
GRID_H = 24
GRID_W = 8


EPSILON = 1e-06


def layer_norm(inputs):
    average = jnp.mean(inputs, axis=-1, keepdims=True)
    centred = inputs - average
    variance = jnp.mean(centred * centred, axis=-1, keepdims=True)
    return centred * lax.rsqrt(variance + EPSILON)


def head_norm(inputs, gain_table):
    mean_square = jnp.mean(inputs * inputs, axis=-1, keepdims=True)
    return inputs * lax.rsqrt(mean_square + EPSILON) * gain_table


def frequencies(pair_count):
    return jnp.power(10000.0, -jnp.arange(pair_count, dtype=jnp.float32) / pair_count)


def rope_angles(cell_ids):
    sixth_part = HEAD_DIM // 6
    time_pairs = HEAD_DIM // 2 - 2 * sixth_part
    plane_cells = GRID_H * GRID_W
    frame_index = (cell_ids // plane_cells).astype(jnp.float32)
    row_index = (cell_ids // GRID_W % GRID_H).astype(jnp.float32)
    column = (cell_ids % GRID_W).astype(jnp.float32)
    return jnp.concatenate(
        [
            frame_index[..., None] * frequencies(time_pairs),
            row_index[..., None] * frequencies(sixth_part),
            column[..., None] * frequencies(sixth_part),
        ],
        axis=-1,
    )


def rotate(inputs, angles):
    half_dim = inputs.shape[-1] // 2
    cosine = jnp.cos(angles)[..., None, :]
    sine_part = jnp.sin(angles)[..., None, :]
    lower_half = inputs[..., :half_dim]
    upper_half = inputs[..., half_dim:]
    return jnp.concatenate(
        [
            lower_half * cosine - upper_half * sine_part,
            lower_half * sine_part + upper_half * cosine,
        ],
        axis=-1,
    )


def attend_self(queries, keys_own, values_own):
    factor = 1.0 / math.sqrt(queries.shape[-1])
    token_total = queries.shape[0]

    def one_block(block_queries):
        scores = (
            jnp.einsum("qhd,khd->hqk", block_queries, keys_own, preferred_element_type=jnp.float32)
            * factor
        )
        weights = jnp.exp(scores)
        totals = jnp.sum(weights, axis=-1)
        mixture = jnp.einsum(
            "hqk,khd->qhd",
            weights.astype(jnp.bfloat16),
            values_own,
            preferred_element_type=jnp.float32,
        )
        return (mixture / jnp.transpose(totals)[:, :, None]).astype(jnp.bfloat16)

    blocked = queries.reshape((token_total // token_total, token_total) + queries.shape[1:])
    return lax.map(one_block, blocked).reshape(queries.shape)


def attend_text(queries, keys_own, values_own, length):
    factor = 1.0 / math.sqrt(queries.shape[-1])
    live_mask = (jnp.arange(keys_own.shape[0]) < length).astype(jnp.float32)
    scores = (
        jnp.einsum("qhd,khd->hqk", queries, keys_own, preferred_element_type=jnp.float32) * factor
    )
    weights = jnp.exp(scores) * live_mask
    totals = jnp.sum(weights, axis=-1)
    mixture = jnp.einsum(
        "hqk,khd->qhd", weights.astype(jnp.bfloat16), values_own, preferred_element_type=jnp.float32
    )
    return (mixture / jnp.transpose(totals)[:, :, None]).astype(jnp.bfloat16)


def pack_projected(block_in, cell_map, w_qkv, self_q_gain, self_k_gain, head_count):
    videos, per_video, model_width = block_in.shape
    projected = jnp.dot(
        block_in.reshape(-1, model_width), w_qkv, preferred_element_type=jnp.float32
    )
    projected = projected.reshape(videos, per_video, 3, HEADS, HEAD_DIM)
    angles = rope_angles(cell_map)
    queries = rotate(
        head_norm(projected[:, :, 0], self_q_gain.reshape(HEADS, HEAD_DIM)), angles
    ).astype(jnp.bfloat16)
    keys_all = rotate(
        head_norm(projected[:, :, 1], self_k_gain.reshape(HEADS, HEAD_DIM)), angles
    ).astype(jnp.bfloat16)
    values_all = projected[:, :, 2].astype(jnp.bfloat16)
    packed = jnp.stack([queries, keys_all, values_all], axis=2)
    group_width = model_width // head_count
    packed = packed.reshape(videos, per_video, 3, head_count, group_width).transpose(3, 0, 1, 2, 4)
    return packed.reshape(head_count, videos, per_video, 3 * group_width)


def local(
    hidden,
    latent,
    cell_map,
    text_lengths,
    block_modulation,
    head_modulation,
    step_sizes,
    w_qkv,
    self_q_gain,
    self_k_gain,
    w_out,
    cross_gain,
    cross_wq,
    cross_q_gain,
    text_keys,
    text_values,
    cross_wo,
    head_w,
):
    head_count = lax.axis_size("head")
    tile_count = lax.axis_size("tile")
    videos, per_video, model_width = hidden.shape
    group_heads = HEADS // head_count
    group_width = group_heads * HEAD_DIM
    stream = hidden.astype(jnp.float32)
    block_shift = block_modulation[:, 0][:, None, :]
    block_scale = block_modulation[:, 1][:, None, :]
    block_gate = block_modulation[:, 2][:, None, :]
    block_in = (layer_norm(stream) * (1.0 + block_scale) + block_shift).astype(jnp.bfloat16)
    packed = pack_projected(block_in, cell_map, w_qkv, self_q_gain, self_k_gain, head_count)
    arrived = lax.all_to_all(
        packed.reshape(head_count * videos, per_video, 3 * group_width),
        ("head", "tile"),
        split_axis=0,
        concat_axis=0,
        tiled=True,
    )
    arrived = arrived.reshape(-1, 3, group_heads, HEAD_DIM)
    own_queries = arrived[:, 0]
    own_keys = arrived[:, 1]
    own_values = arrived[:, 2]
    own_mixture = attend_self(own_queries, own_keys, own_values)
    returned = lax.all_to_all(
        own_mixture.reshape(head_count * tile_count, per_video, group_width),
        ("head", "tile"),
        split_axis=0,
        concat_axis=0,
        tiled=True,
    )
    attended = (
        returned.reshape(head_count, videos, per_video, group_width)
        .transpose(1, 2, 0, 3)
        .reshape(videos * per_video, model_width)
    )
    self_update = jnp.dot(attended, w_out, preferred_element_type=jnp.float32).reshape(
        videos, per_video, model_width
    )
    after_self = stream + block_gate * self_update
    cross_in = (layer_norm(after_self) * cross_gain).astype(jnp.bfloat16)
    copies = jnp.broadcast_to(cross_in[None], (head_count,) + cross_in.shape).reshape(
        head_count * videos, per_video, model_width
    )
    owner_cross = lax.all_to_all(copies, ("head", "tile"), split_axis=0, concat_axis=0, tiled=True)
    owner_cross = owner_cross.reshape(-1, model_width)
    cross_queries = jnp.dot(owner_cross, cross_wq, preferred_element_type=jnp.float32).reshape(
        -1, group_heads, HEAD_DIM
    )
    cross_queries = head_norm(cross_queries, cross_q_gain.reshape(group_heads, HEAD_DIM)).astype(
        jnp.bfloat16
    )
    own_text_keys = text_keys[0].reshape(-1, group_heads, HEAD_DIM)
    own_text_values = text_values[0].reshape(-1, group_heads, HEAD_DIM)
    cross_mixture = attend_text(
        cross_queries, own_text_keys, own_text_values, text_lengths[0]
    ).reshape(-1, group_width)
    summed = lax.psum_scatter(
        jnp.dot(cross_mixture, cross_wo, preferred_element_type=jnp.float32).astype(jnp.bfloat16),
        "head",
        scatter_dimension=0,
        tiled=True,
    )
    cross_out = summed.reshape(tile_count, per_video, model_width)
    returned_cross = lax.all_to_all(cross_out, "tile", split_axis=0, concat_axis=0, tiled=True)
    after_cross = after_self + returned_cross.astype(jnp.float32)
    hidden_next = after_cross.astype(jnp.bfloat16)
    head_shift = head_modulation[:, 0][:, None, :]
    head_scale = head_modulation[:, 1][:, None, :]
    head_in = (layer_norm(after_cross) * (1.0 + head_scale) + head_shift).astype(jnp.bfloat16)
    velocity = jnp.dot(
        head_in.reshape(-1, model_width), head_w, preferred_element_type=jnp.float32
    ).reshape(videos, per_video, -1)
    latent_next = latent + step_sizes[:, None, None] * velocity
    return (hidden_next, latent_next)


def solution(mesh):
    return jax.shard_map(
        local,
        mesh=mesh,
        in_specs=(
            P(None, ("head", "tile"), None),
            P(None, ("head", "tile"), None),
            P(None, ("head", "tile")),
            P("tile"),
            P(),
            P(),
            P(),
            P(),
            P(),
            P(),
            P(),
            P(),
            P(None, "head"),
            P("head"),
            P("tile", None, "head"),
            P("tile", None, "head"),
            P("head", None),
            P(),
        ),
        out_specs=(P(None, ("head", "tile"), None), P(None, ("head", "tile"), None)),
        check_vma=False,
    )
```

profile of v0, /device:TPU:0, one launch (start us, length us, event | category | flops | bytes accessed | tf_op | source)
XLA Modules:
  0.0 215.4 jit_solution(10873028885907284533)
XLA Ops:
  7.2 0.9 slice_bitcast_fusion.3
  8.2 1.1 convert_reduce_fusion
  9.3 1.2 fusion.24
  10.6 18.7 %copy.60 = bf16[1536,4608]{0,1:T(8,128)(2,1)} copy(bf16[1536,4608]{1,0:T(8,128)(2,1)} %param.25) | data formatting | bytes 28311552 | tf_op args[7]
  29.2 8.0 %fusion.33 = f32[8,12,3,12,128]{4,1,3,2,0:T(8,128)S(1)} fusion(bf16[3,12,128,1536,1]{3,2,1,0,4:T(8,128)(2,1)} %bitcast.114, bf16[8,12,1536]{2,0,1:T(8,128)(2,1)S(1)} %copy-done.1, f32[8,1536]{1,0:T(8,128)S(1)} %get-tuple-element.39, f32[8,1536]{1,0:T(8,128)S(1)} %get-tuple-element.40, f32[8,12]{1,0:T(8,128)S(1)} %add_rsqrt_fusion.5, ...), kind=kOutput, calls=%fused_computation.54 | convolution fusion | flops 1359839232 | bytes 16319232 | tf_op jit(solution)/shard_map/dot_general | solution.py:104
  37.2 0.5 multiply_reduce_fusion.3
  37.7 0.1 slice.109
  37.8 0.1 copy-done.11
  38.0 0.1 broadcast_multiply_fusion.2
  38.0 0.1 broadcast_multiply_fusion.1
  38.1 0.3 fusion.63
  38.5 0.5 multiply_multiply_fusion.1
  39.0 0.6 fusion.28
  39.6 0.2 pad_maximum_fusion
  39.9 0.1 copy.62
  40.0 0.9 convert_element_type.85
  40.9 0.2 pad_maximum_fusion.1
  41.1 0.1 copy.63
  41.2 0.2 convert_element_type.86
  41.5 0.1 copy.64
  41.6 0.2 stack.8
  41.8 0.3 copy-done.3
  42.1 0.7 maximum_bitcast_fusion
  42.8 1.8 copy.88
  44.6 2.6 %reshape.204 = bf16[32,12,1152]{2,1,0:T(8,128)(2,1)S(1)} reshape(bf16[4,8,12,3,384]{4,3,2,1,0:T(4,128)(2,1)} %copy.88) | data formatting | bytes 1769472 | tf_op jit(solution)/shard_map/reshape;reshape | solution.py:154
  47.2 37.6 %all_to_all.20 = bf16[32,12,1152]{2,1,0:T(8,128)(2,1)} all-to-all(bf16[32,12,1152]{2,1,0:T(8,128)(2,1)S(1)} %reshape.204), channel_id=1, replica_groups=mesh['head'=4,'tile'=8] {'head','tile'}, dimensions={0} | all-to-all | bytes 1769472 | tf_op jit(solution)/shard_map/all_to_all | solution.py:153
  84.8 2.7 %reshape.193 = bf16[384,3,3,128]{3,2,1,0:T(4,128)(2,1)S(1)} reshape(bf16[32,12,1152]{2,1,0:T(8,128)(2,1)} %all_to_all.20) | data formatting | bytes 1769472 | tf_op jit(solution)/shard_map/reshape | solution.py:160
  87.5 1.1 fusion.64
  88.6 0.3 copy.91
  88.9 1.4 fusion.10
  90.4 0.4 fusion.15
  90.8 0.2 copy.71
  91.1 0.3 reshape_reshape.7
  91.4 15.6 %all_to_all.21 = bf16[32,12,384]{2,1,0:T(8,128)(2,1)S(1)} all-to-all(bf16[32,12,384]{2,1,0:T(8,128)(2,1)S(1)} %reshape_reshape.7), channel_id=1, replica_groups=mesh['head'=4,'tile'=8] {'head','tile'}, dimensions={0} | all-to-all | bytes 589824 | tf_op jit(solution)/shard_map/all_to_all | solution.py:165
  106.9 0.2 copy.121
  107.2 0.1 dot_general.44
  107.3 3.3 %fusion.66 = (f32[8,12]{1,0:T(8,128)S(1)}, f32[8,12,1536]{2,1,0:T(8,128)S(1)}) fusion(bf16[1536,1536]{1,0:T(8,128)(2,1)} %param.28, bf16[8,12,1536]{2,0,1:T(8,128)(2,1)S(1)} %dot_general.44, f32[8,1536]{1,0:T(8,128)S(1)} %get-tuple-element.38, bf16[8,12,1536]{2,0,1:T(8,128)(2,1)S(1)} %copy-done.1), kind=kOutput, calls=%fused_computation.121 | convolution fusion | flops 453574560 | bytes 5947776 | tf_op jit(solution)/shard_map/dot_general | solution.py:177
  110.7 0.2 multiply_reduce_fusion.1
  110.9 0.2 multiply_convert_fusion
  111.1 1.3 broadcast_in_dim.5
  112.4 2.7 %all-to-all-start.2 = ((bf16[32,12,1536]{2,1,0:T(8,128)(2,1)}), bf16[32,12,1536]{2,1,0:T(8,128)(2,1)S(1)}, u32[]{:S(2)}, u32[]{:S(2)}) async-start(bf16[32,12,1536]{2,1,0:T(8,128)(2,1)} %bitcast.115), calls=%async_computation.2 | async-start | bytes 3145728 | tf_op jit(solution)/shard_map/all_to_all | solution.py:185
  115.1 0.0 reduce-scatter.2.cloned.1.call-start
  115.2 2.4 %copy.74 = bf16[1536,384]{0,1:T(8,128)(2,1)} copy(bf16[1536,384]{1,0:T(8,128)(2,1)} %param.30) | data formatting | bytes 2359296 | tf_op args[12]
  118.2 1.9 copy.75
  120.1 1.9 copy.78
  122.1 31.9 %all-to-all-done.2 = bf16[32,12,1536]{2,1,0:T(8,128)(2,1)S(1)} async-done(((bf16[32,12,1536]{2,1,0:T(8,128)(2,1)}), bf16[32,12,1536]{2,1,0:T(8,128)(2,1)S(1)}, u32[]{:S(2)}, u32[]{:S(2)}) %all-to-all-start.2) | async-done | bytes 1179680 | tf_op jit(solution)/shard_map/all_to_all | solution.py:185
  154.0 1.1 reshape.202
  155.1 2.5 %multiply_reduce_fusion.4 = (f32[384,3]{0,1:T(4,128)S(1)}, f32[384,3,128]{0,2,1:T(8,128)S(1)}) fusion(bf16[384,1536,1]{1,0,2:T(8,128)(2,1)} %reshape.202, bf16[3,128,1536]{2,1,0:T(8,128)(2,1)} %bitcast.118), kind=kOutput, calls=%fused_computation.48 | convolution fusion | flops 453278592 | bytes 2953728 | tf_op jit(solution)/shard_map/dot_general | solution.py:187
  157.7 0.8 fusion.8
  158.5 0.1 copy-done.4
  158.6 0.6 fusion.14
  159.2 1.8 convolution_convert_fusion
  161.0 0.0 reduce-scatter.2.cloned.1.call-update
  161.0 26.3 %reduce-scatter.2.cloned.1.call-done = bf16[96,1536]{1,0:T(8,128)(2,1)} async-done(((bf16[384,1536]{1,0:T(8,128)(2,1)}), bf16[96,1536]{1,0:T(8,128)(2,1)}) %reduce-scatter.2.cloned.1.call-update) | async-done | bytes 294928 | tf_op jit(solution)/shard_map/reduce_scatter | solution.py:198
  187.3 1.8 reshape.198
  189.1 4.6 %all-to-all-start.3 = ((bf16[8,12,1536]{2,1,0:T(8,128)(2,1)}), bf16[8,12,1536]{2,1,0:T(8,128)(2,1)S(1)}, u32[]{:S(2)}, u32[]{:S(2)}) async-start(bf16[8,12,1536]{2,1,0:T(8,128)(2,1)} %reshape.198), calls=%async_computation.4 | async-start | bytes 786432 | tf_op jit(solution)/shard_map/all_to_all | solution.py:205
  193.7 0.1 fusion.65
  193.8 12.4 %all-to-all-done.3 = bf16[8,12,1536]{2,1,0:T(8,128)(2,1)S(1)} async-done(((bf16[8,12,1536]{2,1,0:T(8,128)(2,1)}), bf16[8,12,1536]{2,1,0:T(8,128)(2,1)S(1)}, u32[]{:S(2)}, u32[]{:S(2)}) %all-to-all-start.3) | async-done | bytes 294944 | tf_op jit(solution)/shard_map/all_to_all | solution.py:205
  206.2 0.2 fusion.50
  206.4 0.3 multiply_reduce_fusion
  206.7 0.0 copy-done.7
  206.7 0.3 fusion.19
  207.0 0.6 copy.83
  207.7 0.9 copy.82
  (37 shorter events, 0.2 us)
Async XLA Ops:
  7.2 152.0 %copy-start = (bf16[384,1536]{1,0:T(8,128)(2,1)S(1)}, bf16[384,1536]{1,0:T(8,128)(2,1)}, u32[]{:S(2)}) copy-start(bf16[384,1536]{1,0:T(8,128)(2,1)} %param.34) | copy-start | bytes 3538948
  10.5 18.7 %copy-start.1 = (bf16[8,12,1536]{2,0,1:T(8,128)(2,1)S(1)}, bf16[8,12,1536]{2,0,1:T(8,128)(2,1)}, u32[]{:S(2)}) copy-start(bf16[8,12,1536]{2,0,1:T(8,128)(2,1)} %param.18) | copy-start | bytes 884740
  37.2 0.7 copy-start.11
  37.2 1.3 copy-start.8
  37.2 1.3 copy-start.9
  41.1 1.0 copy-start.3
  107.3 3.6 %copy-start.10 = (f32[1536]{0:T(1024)S(1)}, f32[1536]{0:T(1024)}, u32[]{:S(2)}) copy-start(f32[1536]{0:T(1024)} %param.29) | copy-start | bytes 18436
  112.4 41.6 %all-to-all-start.2 = ((bf16[32,12,1536]{2,1,0:T(8,128)(2,1)}), bf16[32,12,1536]{2,1,0:T(8,128)(2,1)S(1)}, u32[]{:S(2)}, u32[]{:S(2)}) async-start(bf16[32,12,1536]{2,1,0:T(8,128)(2,1)} %bitcast.115), calls=%async_computation.2 | async-start | bytes 3145728 | tf_op jit(solution)/shard_map/all_to_all | solution.py:185
  115.1 72.2 %reduce-scatter.2.cloned.1.call-start = ((), (), s32[]{:S(2)}) async-start(), calls=%async_computation.5 | async-start | bytes 1474560 | tf_op jit(solution)/shard_map/reduce_scatter | solution.py:198
  155.1 2.5 %copy-start.2 = (bf16[1,512,384]{1,2,0:T(8,128)(2,1)S(1)}, bf16[1,512,384]{1,2,0:T(8,128)(2,1)}, u32[]{:S(2)}) copy-start(bf16[1,512,384]{1,2,0:T(8,128)(2,1)} %copy.75) | copy-start | bytes 1179652
  155.1 2.5 %copy-start.12 = (f32[384]{0:T(512)S(1)}, f32[384]{0:T(512)}, u32[]{:S(2)}) copy-start(f32[384]{0:T(512)} %param.31) | copy-start | bytes 4612
  157.6 1.0 copy-start.4
  161.0 32.7 %copy-start.6 = (f32[8,2,1536]{2,1,0:T(2,128)S(1)}, f32[8,2,1536]{2,1,0:T(2,128)}, u32[]{:S(2)}) copy-start(f32[8,2,1536]{2,1,0:T(2,128)} %param.23) | copy-start | bytes 294916
  189.1 17.1 %all-to-all-start.3 = ((bf16[8,12,1536]{2,1,0:T(8,128)(2,1)}), bf16[8,12,1536]{2,1,0:T(8,128)(2,1)S(1)}, u32[]{:S(2)}, u32[]{:S(2)}) async-start(bf16[8,12,1536]{2,1,0:T(8,128)(2,1)} %reshape.198), calls=%async_computation.4 | async-start | bytes 786432 | tf_op jit(solution)/shard_map/all_to_all | solution.py:205
  193.7 13.0 %copy-start.5 = (bf16[1536,64]{0,1:T(8,128)(2,1)S(1)}, bf16[1536,64]{0,1:T(8,128)(2,1)}, u32[]{:S(2)}) copy-start(bf16[1536,64]{0,1:T(8,128)(2,1)} %param.35) | copy-start | bytes 589828
  193.7 13.0 %copy-start.7 = (f32[8,12,64]{2,0,1:T(8,128)S(1)}, f32[8,12,64]{2,0,1:T(8,128)}, u32[]{:S(2)}) copy-start(f32[8,12,64]{2,0,1:T(8,128)} %param.19) | copy-start | bytes 73732
  193.7 13.0 %copy-start.13 = (f32[8]{0:T(128)S(1)}, f32[8]{0:T(128)}, u32[]{:S(2)}) copy-start(f32[8]{0:T(128)} %param.24) | copy-start | bytes 100
Sparse Core Ops, SparseCore 0:
  161.2 26.1 reduce-scatter.1
where the time goes:
time: 217 us; the launch traced here: 215 us
  waiting for transfers between devices  70.6 us (33%)
  blocking collectives  53.2 us (25%)
  local copies, waits for them, and re-layouts  42.4 us (20%)
  matrix products  19.2 us (9%)
  between operations  15.1 us (7%)
  other arithmetic  7.52 us (3%)
  starting transfers between devices  7.31 us (3%)
    all_to_all x1, blocking collectives, local(): lax.all_to_all(packed.reshape(head_count * videos, per_video, 3 * group_w...  37.6 us
    all_to_all x1, waiting for transfers between devices, local(): lax.all_to_all(copies, ('head', 'tile'), split_axis=0, concat_axis=0, til...  31.9 us
    unnamed x35, local copies, waits for them, and re-layouts  27.3 us
    reduce_scatter x1, waiting for transfers between devices, local(): lax.psum_scatter(jnp.dot(cross_mixture, cross_wo, preferred_element_type=...  26.3 us
    all_to_all x1, blocking collectives, local(): lax.all_to_all(own_mixture.reshape(head_count * tile_count, per_video, gr...  15.6 us
    all_to_all x1, waiting for transfers between devices, local(): lax.all_to_all(cross_out, 'tile', split_axis=0, concat_axis=0, tiled=True)  12.4 us
    dot_general x1, matrix products, pack_projected(): jnp.dot(block_in.reshape(-1, model_width), w_qkv, preferred_element_type=...  7.98 us
    all_to_all x1, starting transfers between devices, local(): lax.all_to_all(cross_out, 'tile', split_axis=0, concat_axis=0, tiled=True)  4.58 us
  transfers between devices with their start and end apart: 3, of which 3 were waited for; matrix products, arithmetic and copies ran while one was open for 3% of the time, Pallas kernels for 0%

commit v1 on v0

v1 whole, which is shorter than its diff:
```python
import functools
import math

import jax
import jax.numpy as jnp
from jax import lax
from jax.experimental import pallas as pl
from jax.experimental.pallas import tpu as pltpu
from jax.sharding import PartitionSpec as P

HEADS = 12
HEAD_DIM = 128
GRID_H = 24
GRID_W = 8
PAD_ROWS = 16
EXTRA = 128
EPSILON = 1e-06
MESH = pl.DeviceIdType.MESH
F32 = jnp.float32
BF16 = jnp.bfloat16


def frequencies(pair_count):
    return jnp.power(10000.0, -jnp.arange(pair_count, dtype=jnp.float32) / pair_count)


def layer_norm(inputs):
    average = jnp.mean(inputs, axis=-1, keepdims=True)
    centred = inputs - average
    variance = jnp.mean(centred * centred, axis=-1, keepdims=True)
    return centred * lax.rsqrt(variance + EPSILON)


def head_norm(inputs, gain_row):
    mean_square = jnp.mean(inputs * inputs, axis=-1, keepdims=True)
    return inputs * lax.rsqrt(mean_square + EPSILON) * gain_row


def matmul(a, b):
    return jnp.dot(a, b, preferred_element_type=F32)


def matmul_t(a, b):
    return lax.dot_general(a, b, (((1,), (1,)), ((), ())), preferred_element_type=F32)


def kernel(
    tiles,
    per_video,
    ext_ref,
    length_ref,
    block_mod_ref,
    head_mod_ref,
    w_qkv_ref,
    q_gain_ref,
    k_gain_ref,
    w_out_ref,
    cross_gain_ref,
    wq_ref,
    cross_q_gain_ref,
    text_k_ref,
    text_v_ref,
    wo_ref,
    head_w_ref,
    freq_ref,
    hidden_out,
    velocity_out,
    rx,
    stream,
    gathered,
    q_buf,
    k_buf,
    v_buf,
    att_out,
    att_in,
    cross_in,
    part_out,
    part_in,
    own_part,
    next_rows,
    back_out,
    vel_rows,
    vel_out,
    back_in,
    vel_in,
    w_qkv,
    w_out,
    wq,
    wo,
    text_k,
    text_v,
    head_w,
    block_mod,
    head_mod,
    load_sem,
    s1_send,
    s1_recv,
    xy_send,
    xy_recv,
    back_send,
    back_recv,
):
    head = lax.axis_index("head")
    tile = lax.axis_index("tile")
    width = wq_ref.shape[0]
    group = wq_ref.shape[1]
    rows = tiles * per_video
    heads_here = group // HEAD_DIM
    factor = 1.0 / math.sqrt(HEAD_DIM)

    def partner(d):
        return lax.rem(head // 2 + d // 2, 2) * 2 + lax.rem(head % 2 + d % 2, 2)

    def tile_at(d):
        return lax.rem(tile + d + tiles, tiles)

    loads = []

    def load(src, dst):
        copy = pltpu.make_async_copy(src, dst, load_sem.at[len(loads)])
        copy.start()
        loads.append(copy)
        return copy

    load_own = load(ext_ref.at[tile], rx.at[tile])
    load_bm = load(block_mod_ref.at[tile], block_mod)
    load_hm = load(head_mod_ref.at[tile], head_mod)
    load_qkv = [
        load(
            w_qkv_ref.at[:, pl.ds(pl.multiple_of(i * width + head * group, 128), group)],
            w_qkv.at[i],
        )
        for i in range(3)
    ]

    barrier = pltpu.get_barrier_semaphore()
    for d in range(1, tiles):
        pl.semaphore_signal(barrier, inc=1, device_id=(head, tile_at(d)), device_id_type=MESH)
    for d in range(1, 4):
        pl.semaphore_signal(barrier, inc=1, device_id=(partner(d), tile), device_id_type=MESH)
    pl.semaphore_wait(barrier, tiles - 1 + 3)

    stage1 = []
    for d in range(1, tiles):
        to = tile_at(d)
        copy = pltpu.make_async_remote_copy(
            src_ref=ext_ref.at[to],
            dst_ref=rx.at[tile],
            send_sem=s1_send.at[d],
            recv_sem=s1_recv.at[d],
            device_id=(head, to),
            device_id_type=MESH,
        )
        copy.start()
        stage1.append(copy)

    load_out = load(w_out_ref, w_out)
    load_wq = load(wq_ref, wq)
    load_tk = load(text_k_ref.at[0], text_k)
    load_tv = load(text_v_ref.at[0], text_v)
    load_wo = load(wo_ref, wo)
    load_hw = load(head_w_ref, head_w)

    load_own.wait()
    for d in range(1, tiles):
        arrival = pltpu.make_async_remote_copy(
            src_ref=ext_ref.at[tile],
            dst_ref=rx.at[tile_at(-d)],
            send_sem=s1_send.at[d],
            recv_sem=s1_recv.at[d],
            device_id=(head, tile_at(-d)),
            device_id_type=MESH,
        )
        arrival.wait_recv()
    for t in range(tiles):
        stream[t * per_video : t * per_video + PAD_ROWS, :] = rx[t].astype(F32)
    load_bm.wait()
    hidden = stream[:rows, :width]
    block_in = layer_norm(hidden) * (1.0 + block_mod[1:2, :]) + block_mod[0:1, :]
    gathered[head, :, :width] = block_in.astype(BF16)
    gathered[head, :, width:] = stream[:rows, width:].astype(BF16)

    def exchange(step, src, dst, d):
        return pltpu.make_async_remote_copy(
            src_ref=src,
            dst_ref=dst,
            send_sem=xy_send.at[step, d],
            recv_sem=xy_recv.at[step, d],
            device_id=(partner(d), tile),
            device_id_type=MESH,
        )

    sends = []
    for d in range(1, 4):
        copy = exchange(0, gathered.at[head], gathered.at[head], d)
        copy.start()
        sends.append(copy)

    for copy in load_qkv:
        copy.wait()
    q_gain = q_gain_ref[head]
    k_gain = k_gain_ref[head]
    lane = lax.broadcasted_iota(jnp.int32, (1, HEAD_DIM), 1)
    sign = jnp.where(lane < HEAD_DIM // 2, -1.0, 1.0)
    for d in range(4):
        slot = partner(d)
        if d > 0:
            exchange(0, gathered.at[slot], gathered.at[slot], d).wait_recv()
        tokens = gathered[slot, :, :width]
        angles = gathered[slot, :, width:].astype(F32) * freq_ref[...]
        cosine = jnp.cos(angles)
        sine = jnp.sin(angles) * sign
        for i, (gain, buf) in enumerate(((q_gain, q_buf), (k_gain, k_buf))):
            raw = matmul(tokens, w_qkv[i])
            for g in range(heads_here):
                cols = slice(g * HEAD_DIM, (g + 1) * HEAD_DIM)
                u = head_norm(raw[:, cols], gain[g : g + 1, :])
                turned = u * cosine + pltpu.roll(u, HEAD_DIM // 2, 1) * sine
                buf[slot, :, cols] = turned.astype(BF16)
        v_buf[slot] = matmul(tokens, w_qkv[2]).astype(BF16)

    for d in (1, 2, 3, 0):
        slot = partner(d)
        for g in range(heads_here):
            cols = slice(g * HEAD_DIM, (g + 1) * HEAD_DIM)
            keys = k_buf[:, :, cols].reshape(4 * rows, HEAD_DIM)
            values = v_buf[:, :, cols].reshape(4 * rows, HEAD_DIM)
            weights = jnp.exp(matmul_t(q_buf[slot, :, cols], keys) * factor)
            total = jnp.sum(weights, axis=-1, keepdims=True)
            mixed = matmul(weights.astype(BF16), values) / total
            att_out[slot, :, cols] = mixed.astype(BF16)
        if d > 0:
            copy = exchange(1, att_out.at[slot], att_in.at[head], d)
            copy.start()
            sends.append(copy)

    load_out.wait()
    update = matmul(att_out[head], w_out[pl.ds(pl.multiple_of(head * group, 128), group), :])
    for d in range(1, 4):
        slot = partner(d)
        exchange(1, att_out.at[slot], att_in.at[slot], d).wait_recv()
        update += matmul(att_in[slot], w_out[pl.ds(pl.multiple_of(slot * group, 128), group), :])
    after_self = stream[:rows, :width] + block_mod[2:3, :] * update
    stream[:rows, :width] = after_self
    cross_in[head] = (layer_norm(after_self) * cross_gain_ref[...]).astype(BF16)
    for d in range(1, 4):
        copy = exchange(2, cross_in.at[head], cross_in.at[head], d)
        copy.start()
        sends.append(copy)

    for copy in (load_wq, load_tk, load_tv, load_wo):
        copy.wait()
    position = lax.broadcasted_iota(jnp.int32, (1, text_k.shape[0]), 1)
    live = jnp.where(position < length_ref[0], 1.0, 0.0)
    for d in range(4):
        slot = partner(d)
        if d > 0:
            exchange(2, cross_in.at[slot], cross_in.at[slot], d).wait_recv()
        raw = matmul(cross_in[slot], wq[...])
        mixes = []
        for g in range(heads_here):
            cols = slice(g * HEAD_DIM, (g + 1) * HEAD_DIM)
            query = head_norm(raw[:, cols], cross_q_gain_ref[g : g + 1, :]).astype(BF16)
            weights = jnp.exp(matmul_t(query, text_k[:, cols]) * factor) * live
            total = jnp.sum(weights, axis=-1, keepdims=True)
            mixes.append((matmul(weights.astype(BF16), text_v[:, cols]) / total).astype(BF16))
        product = matmul(jnp.concatenate(mixes, axis=-1), wo[...])
        if d == 0:
            own_part[...] = product
        else:
            part_out[d - 1] = product.astype(BF16)
            copy = exchange(3, part_out.at[d - 1], part_in.at[d - 1], d)
            copy.start()
            sends.append(copy)

    total = own_part[...]
    for d in range(1, 4):
        exchange(3, part_out.at[d - 1], part_in.at[d - 1], d).wait_recv()
        total += part_in[d - 1].astype(F32)
    after_cross = stream[:rows, :width] + total.astype(BF16).astype(F32)
    next_rows[:rows, :] = after_cross
    next_rows[rows:, :] = jnp.zeros((PAD_ROWS, width), F32)
    for t in range(tiles):
        back_out[t] = next_rows[t * per_video : t * per_video + PAD_ROWS, :].astype(BF16)

    def giving(kind, src, dst, d):
        return pltpu.make_async_remote_copy(
            src_ref=src,
            dst_ref=dst,
            send_sem=back_send.at[kind, d],
            recv_sem=back_recv.at[kind, d],
            device_id=(head, tile_at(d)),
            device_id_type=MESH,
        )

    for d in range(1, tiles):
        copy = giving(0, back_out.at[tile_at(d)], back_in.at[tile], d)
        copy.start()
        sends.append(copy)
    load_hm.wait()
    load_hw.wait()
    head_in = layer_norm(after_cross) * (1.0 + head_mod[1:2, :]) + head_mod[0:1, :]
    vel_rows[...] = jnp.zeros_like(vel_rows)
    vel_rows[:rows, : head_w.shape[1]] = matmul(head_in.astype(BF16), head_w[...])
    for t in range(tiles):
        vel_out[t] = vel_rows[t * per_video : t * per_video + PAD_ROWS, :]
    for d in range(1, tiles):
        copy = giving(1, vel_out.at[tile_at(d)], vel_in.at[tile], d)
        copy.start()
        sends.append(copy)
    hidden_out[tile] = back_out[tile]
    velocity_out[tile] = vel_out[tile]
    for d in range(1, tiles):
        source = tile_at(-d)
        giving(0, back_out.at[source], back_in.at[source], d).wait_recv()
        hidden_out[source] = back_in[source]
    for d in range(1, tiles):
        source = tile_at(-d)
        giving(1, vel_out.at[source], vel_in.at[source], d).wait_recv()
        velocity_out[source] = vel_in[source]
    for copy in stage1 + sends:
        copy.wait_send()


def local(
    hidden,
    latent,
    cell_map,
    text_lengths,
    block_modulation,
    head_modulation,
    step_sizes,
    w_qkv,
    self_q_gain,
    self_k_gain,
    w_out,
    cross_gain,
    cross_wq,
    cross_q_gain,
    text_keys,
    text_values,
    cross_wo,
    head_w,
):
    head_count = lax.axis_size("head")
    tiles = lax.axis_size("tile")
    videos, per_video, width = hidden.shape
    group = width // head_count
    heads_here = group // HEAD_DIM
    rows = tiles * per_video
    text = text_keys.shape[1]
    channels = head_w.shape[1]
    sixth = HEAD_DIM // 6
    time_pairs = HEAD_DIM // 2 - 2 * sixth

    lane = jnp.arange(EXTRA) % (HEAD_DIM // 2)
    cells = cell_map[..., None]
    places = jnp.where(
        lane < time_pairs,
        cells // (GRID_H * GRID_W),
        jnp.where(lane < time_pairs + sixth, cells // GRID_W % GRID_H, cells % GRID_W),
    ).astype(BF16)
    half = jnp.concatenate([frequencies(time_pairs), frequencies(sixth), frequencies(sixth)])
    freq = jnp.concatenate([half, half])[None, :]
    ext = jnp.pad(
        jnp.concatenate([hidden, places], axis=-1),
        ((0, 0), (0, PAD_ROWS - per_video), (0, 0)),
    )
    any_spec = pl.BlockSpec(memory_space=pl.ANY)
    vmem = pl.BlockSpec(memory_space=pltpu.VMEM)
    smem = pl.BlockSpec(memory_space=pltpu.SMEM)
    dma = pltpu.SemaphoreType.DMA
    hidden_pad, velocity = pl.pallas_call(
        functools.partial(kernel, tiles, per_video),
        out_shape=(
            jax.ShapeDtypeStruct((tiles, PAD_ROWS, width), BF16),
            jax.ShapeDtypeStruct((tiles, PAD_ROWS, 128), F32),
        ),
        in_specs=[
            any_spec,
            smem,
            any_spec,
            any_spec,
            any_spec,
            vmem,
            vmem,
            any_spec,
            vmem,
            any_spec,
            vmem,
            any_spec,
            any_spec,
            any_spec,
            any_spec,
            vmem,
        ],
        out_specs=(vmem, vmem),
        scratch_shapes=[
            pltpu.VMEM((tiles, PAD_ROWS, width + EXTRA), BF16),
            pltpu.VMEM((rows + PAD_ROWS, width + EXTRA), F32),
            pltpu.VMEM((head_count, rows, width + EXTRA), BF16),
            pltpu.VMEM((head_count, rows, group), BF16),
            pltpu.VMEM((head_count, rows, group), BF16),
            pltpu.VMEM((head_count, rows, group), BF16),
            pltpu.VMEM((head_count, rows, group), BF16),
            pltpu.VMEM((head_count, rows, group), BF16),
            pltpu.VMEM((head_count, rows, width), BF16),
            pltpu.VMEM((3, rows, width), BF16),
            pltpu.VMEM((3, rows, width), BF16),
            pltpu.VMEM((rows, width), F32),
            pltpu.VMEM((rows + PAD_ROWS, width), F32),
            pltpu.VMEM((tiles, PAD_ROWS, width), BF16),
            pltpu.VMEM((rows + PAD_ROWS, 128), F32),
            pltpu.VMEM((tiles, PAD_ROWS, 128), F32),
            pltpu.VMEM((tiles, PAD_ROWS, width), BF16),
            pltpu.VMEM((tiles, PAD_ROWS, 128), F32),
            pltpu.VMEM((3, width, group), BF16),
            pltpu.VMEM((width, width), BF16),
            pltpu.VMEM((width, group), BF16),
            pltpu.VMEM((group, width), BF16),
            pltpu.VMEM((text, group), BF16),
            pltpu.VMEM((text, group), BF16),
            pltpu.VMEM((width, channels), BF16),
            pltpu.VMEM((3, width), F32),
            pltpu.VMEM((2, width), F32),
            dma((12,)),
            dma((tiles,)),
            dma((tiles,)),
            dma((4, 4)),
            dma((4, 4)),
            dma((2, tiles)),
            dma((2, tiles)),
        ],
        compiler_params=pltpu.CompilerParams(
            collective_id=0, has_side_effects=True, vmem_limit_bytes=50 * 1024 * 1024
        ),
    )(
        ext,
        text_lengths,
        block_modulation,
        head_modulation,
        w_qkv,
        self_q_gain.reshape(head_count, heads_here, HEAD_DIM),
        self_k_gain.reshape(head_count, heads_here, HEAD_DIM),
        w_out,
        cross_gain.reshape(1, width),
        cross_wq,
        cross_q_gain.reshape(heads_here, HEAD_DIM),
        text_keys,
        text_values,
        cross_wo,
        head_w,
        freq,
    )
    hidden_next = hidden_pad[:, :per_video]
    latent_next = latent + step_sizes[:, None, None] * velocity[:, :per_video, :channels]
    return (hidden_next, latent_next)


def solution(mesh):
    return jax.shard_map(
        local,
        mesh=mesh,
        in_specs=(
            P(None, ("head", "tile"), None),
            P(None, ("head", "tile"), None),
            P(None, ("head", "tile")),
            P("tile"),
            P(),
            P(),
            P(),
            P(),
            P(),
            P(),
            P(),
            P(),
            P(None, "head"),
            P("head"),
            P("tile", None, "head"),
            P("tile", None, "head"),
            P("head", None),
            P(),
        ),
        out_specs=(P(None, ("head", "tile"), None), P(None, ("head", "tile"), None)),
        check_vma=False,
    )
```

time: 217 us -> 92.9 us (0.43)
  Pallas kernels: 0 us -> 78.2 us
  waiting for transfers between devices: 70.6 us -> 0 us
  blocking collectives: 53.2 us -> 0 us
  local copies, waits for them, and re-layouts: 42.4 us -> 11.8 us
  matrix products: 19.2 us -> 0 us
  between operations: 15.1 us -> 1.34 us
  starting transfers between devices: 7.31 us -> 0 us
  other arithmetic: 7.52 us -> 1 us
    pallas_call x0 -> x1, Pallas kernels: none -> 78.2 us  [local(): pl.pallas_call(functools.partial(kernel, tiles, per_video), out_shape=(ja...]
    all_to_all x2 -> x0, blocking collectives: 53.2 us -> none  [the longest x1 37.6 us: local(): lax.all_to_all(packed.reshape(head_count * videos, per_video, 3 * group_w...]
    all_to_all x2 -> x0, waiting for transfers between devices: 44.3 us -> none  [the longest x1 31.9 us: local(): lax.all_to_all(copies, ('head', 'tile'), split_axis=0, concat_axis=0, til...]
    reduce_scatter x1 -> x0, waiting for transfers between devices: 26.3 us -> none  [local(): lax.psum_scatter(jnp.dot(cross_mixture, cross_wo, preferred_element_type=...]
    dot_general x9 -> x0, matrix products: 19.2 us -> none  [the longest x1 7.98 us: pack_projected(): jnp.dot(block_in.reshape(-1, model_width), w_qkv, preferred_element_type=...]
    unnamed x35 -> x19, local copies, waits for them, and re-layouts: 27.3 us -> 9.58 us
    all_to_all x2 -> x0, starting transfers between devices: 7.27 us -> none  [the longest x1 4.58 us: local(): lax.all_to_all(cross_out, 'tile', split_axis=0, concat_axis=0, tiled=True)]
    another operation x4 -> x0, local copies, waits for them, and re-layouts: 4.87 us -> none  [the longest x2 4.39 us: local(): packed.reshape(head_count * videos, per_video, 3 * group_width)]
  transfers between devices with their start and end apart: 3 -> 0, of which waited for: 3 -> 0; matrix products, arithmetic and copies ran while one was open for 3% -> 0% of each run, Pallas kernels for 0% -> 0%
where the time goes in v1:
time: 92.9 us; the launch traced here: 92.3 us
  Pallas kernels  78.2 us (84%)
  local copies, waits for them, and re-layouts  11.8 us (13%)
  between operations  1.34 us (1%)
  other arithmetic  1 us (1%)
    pallas_call x1, Pallas kernels, local(): pl.pallas_call(functools.partial(kernel, tiles, per_video), out_shape=(ja...  78.2 us
    unnamed x19, local copies, waits for them, and re-layouts  9.58 us

profile of v1, /device:TPU:0, one launch (start us, length us, event | category | flops | bytes accessed | tf_op | source)
XLA Modules:
  0.0 92.3 jit_solution(17916303376925223082)
XLA Ops:
  1.3 0.1 concatenate.9
  1.4 0.7 reshape.59.cross_gain_ref
  2.1 0.7 reshape.57.q_gain_ref
  2.8 0.7 reshape.58.k_gain_ref
  3.5 0.7 add_select_fusion.3
  4.2 0.1 select_convert_fusion
  4.3 1.0 %copy.27.block_mod_ref = f32[8,3,1536]{2,1,0:T(4,128)S(1)} copy(f32[8,3,1536]{2,0,1:T(8,128)} %param.22) | data formatting | bytes 294912 | tf_op args[4]
  5.4 1.1 %copy.26 = bf16[8,12,1536]{2,1,0:T(8,128)(2,1)S(1)} copy(bf16[8,12,1536]{2,0,1:T(8,128)(2,1)} %param.18) | data formatting | bytes 589824 | tf_op args[0]
  6.4 0.1 fusion.2.ext_ref
  6.5 1.1 %copy.28.head_w_ref = bf16[1536,64]{1,0:T(8,128)(2,1)S(1)} copy(bf16[1536,64]{0,1:T(8,128)(2,1)} %param.35) | data formatting | bytes 393216 | tf_op args[17]
  7.7 0.0 copy-start
  7.7 1.3 %copy-done = bf16[1536,384]{1,0:T(8,128)(2,1)S(1)} copy-done((bf16[1536,384]{1,0:T(8,128)(2,1)S(1)}, bf16[1536,384]{1,0:T(8,128)(2,1)}, u32[]{:S(2)}) %copy-start) | copy-done | bytes 1179672
  8.9 0.0 copy-start.1
  8.9 1.0 %copy-done.1 = bf16[1,512,384]{2,1,0:T(8,128)(2,1)S(1)} copy-done((bf16[1,512,384]{2,1,0:T(8,128)(2,1)S(1)}, bf16[1,512,384]{2,1,0:T(8,128)(2,1)}, u32[]{:S(2)}) %copy-start.1) | copy-done | bytes 393240
  9.9 0.0 copy-start.2
  9.9 1.0 %copy-done.2 = bf16[1,512,384]{2,1,0:T(8,128)(2,1)S(1)} copy-done((bf16[1,512,384]{2,1,0:T(8,128)(2,1)S(1)}, bf16[1,512,384]{2,1,0:T(8,128)(2,1)}, u32[]{:S(2)}) %copy-start.2) | copy-done | bytes 393240
  10.9 0.0 copy-start.3
  10.9 0.9 copy-done.3
  11.8 0.0 copy-start.4
  11.8 0.7 copy-done.4
  12.5 0.0 copy-start.5
  12.5 0.0 copy-start.6
  12.5 78.2 %shard_map.185 = (bf16[8,16,1536]{2,1,0:T(8,128)(2,1)S(1)}, f32[8,16,128]{2,1,0:T(8,128)S(1)}) custom-call(bf16[8,16,1664]{2,1,0:T(8,128)(2,1)S(1)} %fusion.2.ext_ref, s32[1]{0:T(128)S(6)} %copy.33.length_ref, f32[8,3,1536]{2,1,0:T(4,128)S(1)} %copy.27.block_mod_ref, f32[8,2,1536]{2,1,0:T(2,128)S(1)} %copy-done.3, bf16[1536,4608]{1,0:T(8,128)(2,1)} %w_qkv_ref.1, ...), custom_call_target="tpu_custom_call" | custom-call | tf_op jit(solution)/shard_map/pallas_call | solution.py:373
  90.7 0.9 copy.30
  91.6 0.0 copy-done.5
  91.6 0.0 copy-done.6
  91.6 0.1 copy_add_fusion
  91.7 0.6 copy.31
  (3 shorter events, 0.0 us)
Async XLA Ops:
  7.7 1.3 %copy-start = (bf16[1536,384]{1,0:T(8,128)(2,1)S(1)}, bf16[1536,384]{1,0:T(8,128)(2,1)}, u32[]{:S(2)}) copy-start(bf16[1536,384]{1,0:T(8,128)(2,1)} %wq_ref.1) | copy-start | bytes 3538948
  8.9 1.0 %copy-start.1 = (bf16[1,512,384]{2,1,0:T(8,128)(2,1)S(1)}, bf16[1,512,384]{2,1,0:T(8,128)(2,1)}, u32[]{:S(2)}) copy-start(bf16[1,512,384]{2,1,0:T(8,128)(2,1)} %text_k_ref.1) | copy-start | bytes 1179652
  9.9 1.0 %copy-start.2 = (bf16[1,512,384]{2,1,0:T(8,128)(2,1)S(1)}, bf16[1,512,384]{2,1,0:T(8,128)(2,1)}, u32[]{:S(2)}) copy-start(bf16[1,512,384]{2,1,0:T(8,128)(2,1)} %text_v_ref.1) | copy-start | bytes 1179652
  10.9 0.9 copy-start.3
  11.8 0.7 copy-start.4
  12.5 79.1 %copy-start.5 = (f32[8,12,64]{2,0,1:T(8,128)S(1)}, f32[8,12,64]{2,0,1:T(8,128)}, u32[]{:S(2)}) copy-start(f32[8,12,64]{2,0,1:T(8,128)} %param.19) | copy-start | bytes 73732
  12.5 79.1 %copy-start.6 = (f32[8]{0:T(128)S(1)}, f32[8]{0:T(128)}, u32[]{:S(2)}) copy-start(f32[8]{0:T(128)} %param.24) | copy-start | bytes 100

commit v2 on v1

v2 whole, which is shorter than its diff:
```python
import functools
import math

import jax
import jax.numpy as jnp
import numpy as np
from jax import lax
from jax.experimental import pallas as pl
from jax.experimental.pallas import tpu as pltpu
from jax.sharding import PartitionSpec as P

HEADS = 12
HEAD_DIM = 128
GRID_H = 24
GRID_W = 8
PAD_ROWS = 16
EXTRA = 128
EPSILON = 1e-06
MESH = pl.DeviceIdType.MESH
F32 = jnp.float32
BF16 = jnp.bfloat16


def frequencies(pair_count):
    return np.power(10000.0, -np.arange(pair_count) / pair_count).astype(np.float32)


def layer_norm(inputs):
    average = jnp.mean(inputs, axis=-1, keepdims=True)
    centred = inputs - average
    variance = jnp.mean(centred * centred, axis=-1, keepdims=True)
    return centred * lax.rsqrt(variance + EPSILON)


def head_norm(inputs, gain_row):
    mean_square = jnp.mean(inputs * inputs, axis=-1, keepdims=True)
    return inputs * lax.rsqrt(mean_square + EPSILON) * gain_row


def matmul(a, b):
    return jnp.dot(a, b, preferred_element_type=F32)


def matmul_t(a, b):
    return lax.dot_general(a, b, (((1,), (1,)), ((), ())), preferred_element_type=F32)


def kernel(
    tiles,
    per_video,
    ext_ref,
    length_ref,
    block_mod_ref,
    head_mod_ref,
    w_qkv_ref,
    w_out_ref,
    wq_ref,
    text_k_ref,
    text_v_ref,
    wo_ref,
    head_w_ref,
    small_ref,
    hidden_out,
    velocity_out,
    rx,
    stream,
    gathered,
    q_buf,
    k_buf,
    v_buf,
    att_out,
    att_in,
    cross_in,
    part_out,
    part_in,
    own_part,
    next_rows,
    back_out,
    vel_rows,
    vel_out,
    back_in,
    vel_in,
    w_qkv,
    w_out,
    wq,
    wo,
    text_k,
    text_v,
    head_w,
    block_mod,
    head_mod,
    load_sem,
    s1_send,
    s1_recv,
    xy_send,
    xy_recv,
    back_send,
    back_recv,
):
    head = lax.axis_index("head")
    tile = lax.axis_index("tile")
    width = wq_ref.shape[0]
    group = wq_ref.shape[1]
    rows = tiles * per_video
    half_tiles = tiles // 2
    half = rows // 2
    near = tile // half_tiles
    far = 1 - near
    inner = lax.rem(tile, half_tiles)
    heads_here = group // HEAD_DIM
    factor = 1.0 / math.sqrt(HEAD_DIM)

    def partner(d):
        return lax.rem(head // 2 + d // 2, 2) * 2 + lax.rem(head % 2 + d % 2, 2)

    def tile_at(d):
        return lax.rem(tile + d + tiles, tiles)

    def tile_in(side, d):
        return side * half_tiles + lax.rem(inner + d + half_tiles, half_tiles)

    reach = [(near, d, half_tiles + d) for d in range(1, half_tiles)]
    beyond = [(far, d, d) for d in range(half_tiles)]

    loads = []

    def load(src, dst):
        copy = pltpu.make_async_copy(src, dst, load_sem.at[len(loads)])
        copy.start()
        loads.append(copy)
        return copy

    load_own = load(ext_ref.at[tile], rx.at[tile])
    load_bm = load(block_mod_ref, block_mod)
    load_hm = load(head_mod_ref.at[tile], head_mod)
    load_qkv = [
        load(
            w_qkv_ref.at[:, pl.ds(pl.multiple_of(i * width + head * group, 128), group)],
            w_qkv.at[i],
        )
        for i in range(3)
    ]

    barrier = pltpu.get_barrier_semaphore()
    for d in range(1, tiles):
        pl.semaphore_signal(barrier, inc=1, device_id=(head, tile_at(d)), device_id_type=MESH)
    for d in range(1, 4):
        pl.semaphore_signal(barrier, inc=1, device_id=(partner(d), tile), device_id_type=MESH)
    pl.semaphore_wait(barrier, tiles - 1 + 3)

    stage1 = []
    for side, d, index in reach + beyond:
        to = tile_in(side, d)
        copy = pltpu.make_async_remote_copy(
            src_ref=ext_ref.at[to],
            dst_ref=rx.at[tile],
            send_sem=s1_send.at[index],
            recv_sem=s1_recv.at[index],
            device_id=(head, to),
            device_id_type=MESH,
        )
        copy.start()
        stage1.append(copy)

    load_out = load(w_out_ref, w_out)
    load_wq = load(wq_ref, wq)
    load_tk = load(text_k_ref.at[0], text_k)
    load_tv = load(text_v_ref.at[0], text_v)
    load_wo = load(wo_ref, wo)
    load_hw = load(head_w_ref, head_w)

    def exchange(step, src, dst, d):
        return pltpu.make_async_remote_copy(
            src_ref=src,
            dst_ref=dst,
            send_sem=xy_send.at[step, d],
            recv_sem=xy_recv.at[step, d],
            device_id=(partner(d), tile),
            device_id_type=MESH,
        )

    load_own.wait()
    load_bm.wait()
    here = pl.ds(tile, 1)
    shift, scale, gate = block_mod[0, here, :], block_mod[1, here, :], block_mod[2, here, :]
    sends = []
    for part, (side, arrivals) in enumerate(((near, reach), (far, beyond))):
        for _, d, index in arrivals:
            source = tile_in(side, -d)
            pltpu.make_async_remote_copy(
                src_ref=ext_ref.at[tile],
                dst_ref=rx.at[source],
                send_sem=s1_send.at[index],
                recv_sem=s1_recv.at[index],
                device_id=(head, source),
                device_id_type=MESH,
            ).wait_recv()
        for j in range(half_tiles):
            block = rx[side * half_tiles + j].astype(F32)
            stream[side, j * per_video : j * per_video + PAD_ROWS, :] = block
        block_in = layer_norm(stream[side, :half, :width]) * (1.0 + scale) + shift
        gathered[head, side, :, :width] = block_in.astype(BF16)
        gathered[head, side, :, width:] = stream[side, :half, width:].astype(BF16)
        for d in range(1, 4):
            block = gathered.at[head, side]
            copy = exchange(part, block, block, d)
            copy.start()
            sends.append(copy)

    for copy in load_qkv:
        copy.wait()
    own_cols = pl.ds(pl.multiple_of(head * group, 128), group)
    q_gain = small_ref[0:1, own_cols]
    k_gain = small_ref[1:2, own_cols]
    lane = lax.broadcasted_iota(jnp.int32, (1, HEAD_DIM), 1)
    sign = jnp.where(lane < HEAD_DIM // 2, -1.0, 1.0)
    for d in range(4):
        slot = partner(d)
        if d > 0:
            for part, side in enumerate((near, far)):
                block = gathered.at[slot, side]
                exchange(part, block, block, d).wait_recv()
        tokens = gathered[slot, :, :, :width].reshape(rows, width)
        places = gathered[slot, :, :, width:].reshape(rows, EXTRA)
        angles = places.astype(F32) * small_ref[4:5, :EXTRA]
        cosine = jnp.cos(angles)
        sine = jnp.sin(angles) * sign
        for i, (gain, buf) in enumerate(((q_gain, q_buf), (k_gain, k_buf))):
            raw = matmul(tokens, w_qkv[i])
            for g in range(heads_here):
                cols = slice(g * HEAD_DIM, (g + 1) * HEAD_DIM)
                u = head_norm(raw[:, cols], gain[:, cols])
                turned = u * cosine + pltpu.roll(u, HEAD_DIM // 2, 1) * sine
                buf[slot, :, cols] = turned.astype(BF16)
        v_buf[slot] = matmul(tokens, w_qkv[2]).astype(BF16)

    for d in (1, 2, 3, 0):
        slot = partner(d)
        for g in range(heads_here):
            cols = slice(g * HEAD_DIM, (g + 1) * HEAD_DIM)
            keys = k_buf[:, :, cols].reshape(4 * rows, HEAD_DIM)
            values = v_buf[:, :, cols].reshape(4 * rows, HEAD_DIM)
            weights = jnp.exp(matmul_t(q_buf[slot, :, cols], keys) * factor)
            total = jnp.sum(weights, axis=-1, keepdims=True)
            mixed = matmul(weights.astype(BF16), values) / total
            att_out[slot, :, cols] = mixed.astype(BF16)
        if d > 0:
            copy = exchange(2, att_out.at[slot], att_in.at[head], d)
            copy.start()
            sends.append(copy)

    load_out.wait()
    update = matmul(att_out[head], w_out[pl.ds(pl.multiple_of(head * group, 128), group), :])
    for d in range(1, 4):
        slot = partner(d)
        exchange(2, att_out.at[slot], att_in.at[slot], d).wait_recv()
        update += matmul(att_in[slot], w_out[pl.ds(pl.multiple_of(slot * group, 128), group), :])
    for side in range(2):
        after_self = stream[side, :half, :width] + gate * update[side * half : (side + 1) * half]
        stream[side, :half, :width] = after_self
        cross_in[head, side] = (layer_norm(after_self) * small_ref[2:3, :]).astype(BF16)
    for part, side in enumerate((far, near)):
        for d in range(1, 4):
            block = cross_in.at[head, side]
            copy = exchange(3 + part, block, block, d)
            copy.start()
            sends.append(copy)

    for copy in (load_wq, load_tk, load_tv, load_wo):
        copy.wait()
    position = lax.broadcasted_iota(jnp.int32, (1, text_k.shape[0]), 1)
    live = jnp.where(position < length_ref[0], 1.0, 0.0)
    for part, side in enumerate((far, near)):
        for d in range(4):
            slot = partner(d)
            if d > 0:
                block = cross_in.at[slot, side]
                exchange(3 + part, block, block, d).wait_recv()
            raw = matmul(cross_in[slot, side], wq[...])
            mixes = []
            for g in range(heads_here):
                cols = slice(g * HEAD_DIM, (g + 1) * HEAD_DIM)
                query = head_norm(raw[:, cols], small_ref[3:4, cols]).astype(BF16)
                weights = jnp.exp(matmul_t(query, text_k[:, cols]) * factor) * live
                total = jnp.sum(weights, axis=-1, keepdims=True)
                mixes.append((matmul(weights.astype(BF16), text_v[:, cols]) / total).astype(BF16))
            product = matmul(jnp.concatenate(mixes, axis=-1), wo[...])
            if d == 0:
                own_part[part] = product
            else:
                part_out[part, d - 1] = product.astype(BF16)
                copy = exchange(5 + part, part_out.at[part, d - 1], part_in.at[part, d - 1], d)
                copy.start()
                sends.append(copy)

    def giving(kind, src, dst, to, index):
        return pltpu.make_async_remote_copy(
            src_ref=src,
            dst_ref=dst,
            send_sem=back_send.at[kind, index],
            recv_sem=back_recv.at[kind, index],
            device_id=(head, to),
            device_id_type=MESH,
        )

    load_hm.wait()
    load_hw.wait()
    next_rows[half:, :] = jnp.zeros((PAD_ROWS, width), F32)
    vel_rows[...] = jnp.zeros_like(vel_rows)
    for part, (side, leaving) in enumerate(((far, beyond), (near, reach))):
        total = own_part[part]
        for d in range(1, 4):
            exchange(
                5 + part, part_out.at[part, d - 1], part_in.at[part, d - 1], d
            ).wait_recv()
            total += part_in[part, d - 1].astype(F32)
        after_cross = stream[side, :half, :width] + total.astype(BF16).astype(F32)
        next_rows[:half, :] = after_cross
        for j in range(half_tiles):
            block = next_rows[j * per_video : j * per_video + PAD_ROWS, :]
            back_out[side * half_tiles + j] = block.astype(BF16)
        for _, d, index in leaving:
            to = tile_in(side, d)
            copy = giving(0, back_out.at[to], back_in.at[tile], to, index)
            copy.start()
            sends.append(copy)
        head_in = layer_norm(after_cross) * (1.0 + head_mod[1:2, :]) + head_mod[0:1, :]
        vel_rows[:half, : head_w.shape[0]] = matmul_t(head_in.astype(BF16), head_w[...])
        for j in range(half_tiles):
            vel_out[side * half_tiles + j] = vel_rows[j * per_video : j * per_video + PAD_ROWS, :]
        for _, d, index in leaving:
            to = tile_in(side, d)
            copy = giving(1, vel_out.at[to], vel_in.at[tile], to, index)
            copy.start()
            sends.append(copy)
    hidden_out[tile] = back_out[tile]
    velocity_out[tile] = vel_out[tile]
    for side, d, index in reach + beyond:
        source = tile_in(side, -d)
        giving(0, back_out.at[source], back_in.at[source], source, index).wait_recv()
        hidden_out[source] = back_in[source]
        giving(1, vel_out.at[source], vel_in.at[source], source, index).wait_recv()
        velocity_out[source] = vel_in[source]
    for copy in stage1 + sends:
        copy.wait_send()


def local(
    hidden,
    latent,
    cell_map,
    text_lengths,
    block_modulation,
    head_modulation,
    step_sizes,
    w_qkv,
    self_q_gain,
    self_k_gain,
    w_out,
    cross_gain,
    cross_wq,
    cross_q_gain,
    text_keys,
    text_values,
    cross_wo,
    head_w,
):
    head_count = lax.axis_size("head")
    tiles = lax.axis_size("tile")
    videos, per_video, width = hidden.shape
    group = width // head_count
    rows = tiles * per_video
    text = text_keys.shape[1]
    channels = head_w.shape[1]
    sixth = HEAD_DIM // 6
    time_pairs = HEAD_DIM // 2 - 2 * sixth

    lane = jnp.arange(EXTRA) % (HEAD_DIM // 2)
    cells = cell_map[..., None]
    places = jnp.where(
        lane < time_pairs,
        cells // (GRID_H * GRID_W),
        jnp.where(lane < time_pairs + sixth, cells // GRID_W % GRID_H, cells % GRID_W),
    ).astype(BF16)
    half = np.concatenate([frequencies(n) for n in (time_pairs, sixth, sixth)])
    freq = np.zeros((width,), np.float32)
    freq[:EXTRA] = np.concatenate([half, half])
    small = jnp.stack(
        [self_q_gain, self_k_gain, cross_gain, jnp.pad(cross_q_gain, (0, width - group)), freq]
    )
    ext = jnp.pad(
        jnp.concatenate([hidden, places], axis=-1),
        ((0, 0), (0, PAD_ROWS - per_video), (0, 0)),
    )
    any_spec = pl.BlockSpec(memory_space=pl.ANY)
    vmem = pl.BlockSpec(memory_space=pltpu.VMEM)
    smem = pl.BlockSpec(memory_space=pltpu.SMEM)
    dma = pltpu.SemaphoreType.DMA
    hidden_pad, velocity = pl.pallas_call(
        functools.partial(kernel, tiles, per_video),
        out_shape=(
            jax.ShapeDtypeStruct((tiles, PAD_ROWS, width), BF16),
            jax.ShapeDtypeStruct((tiles, PAD_ROWS, 128), F32),
        ),
        in_specs=[any_spec, smem] + [any_spec] * 9 + [vmem],
        out_specs=(vmem, vmem),
        scratch_shapes=[
            pltpu.VMEM((tiles, PAD_ROWS, width + EXTRA), BF16),
            pltpu.VMEM((2, rows // 2 + PAD_ROWS, width + EXTRA), F32),
            pltpu.VMEM((head_count, 2, rows // 2, width + EXTRA), BF16),
            pltpu.VMEM((head_count, rows, group), BF16),
            pltpu.VMEM((head_count, rows, group), BF16),
            pltpu.VMEM((head_count, rows, group), BF16),
            pltpu.VMEM((head_count, rows, group), BF16),
            pltpu.VMEM((head_count, rows, group), BF16),
            pltpu.VMEM((head_count, 2, rows // 2, width), BF16),
            pltpu.VMEM((2, 3, rows // 2, width), BF16),
            pltpu.VMEM((2, 3, rows // 2, width), BF16),
            pltpu.VMEM((2, rows // 2, width), F32),
            pltpu.VMEM((rows // 2 + PAD_ROWS, width), F32),
            pltpu.VMEM((tiles, PAD_ROWS, width), BF16),
            pltpu.VMEM((rows // 2 + PAD_ROWS, 128), F32),
            pltpu.VMEM((tiles, PAD_ROWS, 128), F32),
            pltpu.VMEM((tiles, PAD_ROWS, width), BF16),
            pltpu.VMEM((tiles, PAD_ROWS, 128), F32),
            pltpu.VMEM((3, width, group), BF16),
            pltpu.VMEM((width, width), BF16),
            pltpu.VMEM((width, group), BF16),
            pltpu.VMEM((group, width), BF16),
            pltpu.VMEM((text, group), BF16),
            pltpu.VMEM((text, group), BF16),
            pltpu.VMEM((channels, width), BF16),
            pltpu.VMEM((3, videos, width), F32),
            pltpu.VMEM((2, width), F32),
            dma((12,)),
            dma((tiles,)),
            dma((tiles,)),
            dma((7, 4)),
            dma((7, 4)),
            dma((2, tiles)),
            dma((2, tiles)),
        ],
        compiler_params=pltpu.CompilerParams(
            collective_id=0, has_side_effects=True, vmem_limit_bytes=60 * 1024 * 1024
        ),
    )(
        ext,
        text_lengths,
        block_modulation.transpose(1, 0, 2),
        head_modulation,
        w_qkv,
        w_out,
        cross_wq,
        text_keys,
        text_values,
        cross_wo,
        head_w.T,
        small,
    )
    hidden_next = hidden_pad[:, :per_video]
    latent_next = latent + step_sizes[:, None, None] * velocity[:, :per_video, :channels]
    return (hidden_next, latent_next)


def solution(mesh):
    return jax.shard_map(
        local,
        mesh=mesh,
        in_specs=(
            P(None, ("head", "tile"), None),
            P(None, ("head", "tile"), None),
            P(None, ("head", "tile")),
            P("tile"),
            P(),
            P(),
            P(),
            P(),
            P(),
            P(),
            P(),
            P(),
            P(None, "head"),
            P("head"),
            P("tile", None, "head"),
            P("tile", None, "head"),
            P("head", None),
            P(),
        ),
        out_specs=(P(None, ("head", "tile"), None), P(None, ("head", "tile"), None)),
        check_vma=False,
    )
```

time: 92.9 us -> 82.5 us (0.89)
  Pallas kernels: 78.2 us -> 70.4 us
  local copies, waits for them, and re-layouts: 11.8 us -> 7.73 us
  other arithmetic: 1 us -> 2.58 us
    pallas_call x1, Pallas kernels: 78.2 us -> 70.4 us  [local(): pl.pallas_call(functools.partial(kernel, tiles, per_video), out_shape=(ja...]
    unnamed x19 -> x7, local copies, waits for them, and re-layouts: 9.58 us -> 3.57 us
    another operation x0 -> x5, local copies, waits for them, and re-layouts: none -> 3.47 us  [local(): jnp.stack([self_q_gain, self_k_gain, cross_gain, jnp.pad(cross_q_gain, (0...]
    reshape x3 -> x0, local copies, waits for them, and re-layouts: 2.11 us -> none  [the longest x1 0.71 us: local(): cross_gain.reshape(1, width)]
where the time goes in v2:
time: 82.5 us; the launch traced here: 82 us
  Pallas kernels  70.4 us (85%)
  local copies, waits for them, and re-layouts  7.73 us (9%)
  other arithmetic  2.58 us (3%)
  between operations  1.31 us (2%)
    pallas_call x1, Pallas kernels, local(): pl.pallas_call(functools.partial(kernel, tiles, per_video), out_shape=(ja...  70.4 us
    unnamed x7, local copies, waits for them, and re-layouts  3.57 us
    another operation x5, local copies, waits for them, and re-layouts, local(): jnp.stack([self_q_gain, self_k_gain, cross_gain, jnp.pad(cross_q_gain, (0...  3.47 us

profile of v2, /device:TPU:0, one launch (start us, length us, event | category | flops | bytes accessed | tf_op | source)
XLA Modules:
  0.0 82.0 jit_solution(11727254178575040670)
XLA Ops:
  1.3 0.7 stack.18
  2.0 0.7 stack.19
  2.7 0.7 stack.20
  3.4 0.7 pad.9
  4.1 0.7 add_select_fusion.3
  4.8 0.1 select_convert_fusion
  4.9 1.4 %stack.23.small_ref = f32[5,1536]{1,0:T(8,128)} concatenate(f32[1,1536]{1,0:T(1,128)S(1)} %stack.18, f32[1,1536]{1,0:T(1,128)S(1)} %stack.19, f32[1,1536]{1,0:T(1,128)S(1)} %stack.20, f32[1,1536]{1,0:T(1,128)S(1)} %stack.21, f32[1,1536]{1,0:T(1,128)} %constant.79), dimensions={0} | concatenate | bytes 61440 | tf_op jit(solution)/shard_map/stack | solution.py:388
  6.3 1.1 %copy.21 = bf16[8,12,1536]{2,1,0:T(8,128)(2,1)S(1)} copy(bf16[8,12,1536]{2,0,1:T(8,128)(2,1)} %param.19) | data formatting | bytes 589824 | tf_op args[0]
  7.3 0.8 %fusion.2.ext_ref = bf16[8,16,1664]{2,1,0:T(8,128)(2,1)} fusion(bf16[8,12,128]{2,1,0:T(8,128)(2,1)S(1)} %select_convert_fusion, bf16[8,12,1536]{2,1,0:T(8,128)(2,1)S(1)} %copy.21), kind=kLoop, calls=%fused_computation.3 | loop fusion | flops 1490944 | bytes 745472 | tf_op jit(solution)/shard_map/concatenate | solution.py:392
  8.2 0.0 copy-start
  8.2 0.0 copy-start.1
  8.2 70.4 %shard_map.194 = (bf16[8,16,1536]{2,1,0:T(8,128)(2,1)}, f32[8,16,128]{2,1,0:T(8,128)}) custom-call(bf16[8,16,1664]{2,1,0:T(8,128)(2,1)} %fusion.2.ext_ref, s32[1]{0:T(128)S(6)} %copy.26.length_ref, f32[3,8,1536]{2,1,0:T(8,128)} %bitcast.5, f32[8,2,1536]{2,1,0:T(2,128)} %head_mod_ref.1, bf16[1536,4608]{1,0:T(8,128)(2,1)} %w_qkv_ref.1, ...), custom_call_target="tpu_custom_call" | custom-call | tf_op jit(solution)/shard_map/pallas_call | solution.py:399
  78.5 1.9 %copy.23 = bf16[8,12,1536]{2,0,1:T(8,128)(2,1)} copy(bf16[8,12,1536]{2,1,0:T(8,128)(2,1)} %bitcast.3) | data formatting | bytes 589824
  80.4 0.0 copy-done
  80.4 0.0 copy-done.1
  80.4 0.9 %copy_add_fusion = f32[8,12,64]{2,1,0:T(8,128)S(1)} fusion(f32[8,12,64]{2,0,1:T(8,128)S(1)} %copy-done, f32[8,16,128]{2,1,0:T(8,128)} %get-tuple-element.5, f32[8]{0:T(128)S(1)} %copy-done.1), kind=kLoop, calls=%fused_computation.4 | loop fusion | flops 12288 | bytes 73760 | tf_op jit(solution)/shard_map/add | solution.py:461
  81.3 0.6 copy.24
  (2 shorter events, 0.0 us)
Async XLA Ops:
  8.2 72.2 %copy-start = (f32[8,12,64]{2,0,1:T(8,128)S(1)}, f32[8,12,64]{2,0,1:T(8,128)}, u32[]{:S(2)}) copy-start(f32[8,12,64]{2,0,1:T(8,128)} %param.20) | copy-start | bytes 73732
  8.2 72.2 %copy-start.1 = (f32[8]{0:T(128)S(1)}, f32[8]{0:T(128)}, u32[]{:S(2)}) copy-start(f32[8]{0:T(128)} %param.25) | copy-start | bytes 100
